TPU v7x, 32 devices: a whole 2x2x4 slice. The times are simulated.
32 devices in a mesh: wave: 8 (over y, x, core), atom: 4 (over z).
Axes of the slice: x: 2, y: 2, z: 4, core: 2. Of those that a mesh axis runs over, the one named last changes fastest.
Arguments:
- slab: float32 [4096, 512], P('wave', 'atom'), may hold values from -0.09375 to 0.09375
- orbitals: float32 [4096, 256], P('wave'), may hold values from -6 to 6
- sphere_ops: float32 [3, 8, 64, 64], P(None, 'atom'), may hold values from -0.75 to 0.75
- wave_terms: float32 [3, 4096], P(None, 'wave'), may hold values from -1 to 1
Outputs:
- applied: float32 [3, 4096, 256], P(None, ('wave', 'atom'))
All inputs are finite; a program needn't handle non-finite values.
Results may differ from a plain program's by a relative error of at most 0.0001.
Values sent between devices are 32-bit elements; how exact they have to be, the bound alone decides.
A program may use at most 64 MiB of HBM per device.

v0:
```python
import jax
import jax.numpy as jnp
from jax import lax
from jax.sharding import PartitionSpec as P


def shards(slab, orbitals, sphere_ops, wave_terms):
    partial_value = jnp.dot(
        slab.T, orbitals, preferred_element_type=jnp.float32, precision=lax.Precision.HIGHEST
    )
    coeffs = lax.psum(partial_value, "wave")
    atoms_here = sphere_ops.shape[1]
    width = sphere_ops.shape[2]
    blocks = coeffs.reshape(atoms_here, width, coeffs.shape[1])
    inner = jnp.einsum("dalm,amb->dalb", sphere_ops, blocks, precision=lax.Precision.HIGHEST)
    inner = inner.reshape(3, atoms_here * width, coeffs.shape[1])
    own_rows = orbitals.shape[0] // lax.axis_size("atom")
    first_row = lax.axis_index("atom") * own_rows
    own_orbitals = lax.dynamic_slice_in_dim(orbitals, first_row, own_rows, 0)
    own_factors = lax.dynamic_slice_in_dim(wave_terms, first_row, own_rows, 1)
    local_part = own_factors[:, :, None] * own_orbitals[None]
    terms = jnp.einsum("ws,dsb->dwb", slab, inner, precision=lax.Precision.HIGHEST)
    summed = lax.psum_scatter(terms, "atom", scatter_dimension=1, tiled=True)
    return summed + local_part


def solution(mesh):
    return jax.shard_map(
        shards,
        mesh=mesh,
        in_specs=(P("wave", "atom"), P("wave", None), P(None, "atom", None, None), P(None, "wave")),
        out_specs=P(None, ("wave", "atom"), None),
        check_vma=False,
    )
```

profile of v0, /device:TPU:1, one launch (start us, length us, event | category | flops | bytes accessed | tf_op | source)
XLA Modules:
  0.0 113.0 jit_solution(5868753596926525371)
XLA Ops:
  6.5 0.0 copy-start
  6.5 0.0 copy-start.1
  6.5 0.0 all-reduce.2.cloned.1.call-start
  6.5 1.0 copy-done
  7.6 2.2 %fusion.3 = f32[128,256]{1,0:T(8,128)} fusion(f32[512,128]{1,0:T(8,128)} %param.4, f32[512,256]{1,0:T(8,128)S(1)} %copy-done), kind=kOutput, calls=%fused_computation.8 | convolution fusion | flops 201326592 | bytes 917504 | tf_op jit(solution)/shard_map/dot_general | solution.py:8
  9.8 0.0 all-reduce.2.cloned.1.call-update
  9.8 0.0 reduce-scatter.2.cloned.1.call-start
  9.9 54.8 %all-reduce.2.cloned.1.call-done = f32[2,64,256]{2,1,0:T(8,128)} async-done(((f32[2,64,256]{2,1,0:T(8,128)}), f32[2,64,256]{2,1,0:T(8,128)}) %all-reduce.2.cloned.1.call-update) | async-done | bytes 131088 | tf_op jit(solution)/shard_map/psum | solution.py:11
  64.7 1.4 %convolution_bitcast_fusion.1 = f32[3,2,64,256]{3,2,0,1:T(8,128)S(1)} fusion(f32[3,2,64,64]{3,2,1,0:T(8,128)} %param.6, f32[2,64,256]{2,1,0:T(8,128)} %all-reduce.2.cloned.1.call-done), kind=kOutput, calls=%fused_computation.1 | convolution fusion | flops 75497472 | bytes 622592 | tf_op jit(solution)/shard_map/dalm,amb->dalb/dot_general | solution.py:15
  66.1 0.0 copy-done.1
  66.2 2.6 %convolution_bitcast_fusion = f32[3,512,256]{1,2,0:T(8,128)} fusion(f32[3,128,256]{2,1,0:T(8,128)S(1)} %bitcast.17, f32[512,128]{1,0:T(8,128)S(1)} %copy-done.1), kind=kOutput, calls=%fused_computation | convolution fusion | flops 603979776 | bytes 2228224 | tf_op jit(solution)/shard_map/ws,dsb->dwb/dot_general | solution.py:22
  68.8 0.0 reduce-scatter.2.cloned.1.call-update
  68.8 0.1 copy.11
  68.9 0.7 constant_dynamic-slice_fusion.1
  69.6 34.6 %reduce-scatter.2.cloned.1.call-done = f32[3,128,256]{1,2,0:T(8,128)} async-done(((f32[3,512,256]{1,2,0:T(8,128)}), f32[3,128,256]{1,2,0:T(8,128)}) %reduce-scatter.2.cloned.1.call-update) | async-done | bytes 393232 | tf_op jit(solution)/shard_map/reduce_scatter | solution.py:23
  104.2 1.0 multiply_add_fusion
  105.3 0.9 copy.12
  (2 shorter events, 0.0 us)
Async XLA Ops:
  6.5 1.0 copy-start
  6.5 59.6 %copy-start.1 = (f32[512,128]{1,0:T(8,128)S(1)}, f32[512,128]{1,0:T(8,128)}, u32[]{:S(2)}) copy-start(f32[512,128]{1,0:T(8,128)} %param.4) | copy-start | bytes 786436
  6.5 58.1 %all-reduce.2.cloned.1.call-start = ((), (), s32[]{:S(2)}) async-start(), calls=%async_computation.1 | async-start | bytes 262144 | tf_op jit(solution)/shard_map/psum | solution.py:11
  9.8 94.4 %reduce-scatter.2.cloned.1.call-start = ((), (), s32[]{:S(2)}) async-start(), calls=%async_computation.2 | async-start | bytes 1966080 | tf_op jit(solution)/shard_map/reduce_scatter | solution.py:23
Sparse Core Ops, SparseCore 0:
  10.4 54.2 all-reduce.1
  68.9 35.2 reduce-scatter.1
where the time goes:
time: 114 us; the launch traced here: 113 us
  waiting for transfers between devices  89.4 us (78%)
  between operations  13.4 us (12%)
  matrix products  6.27 us (6%)
  local copies, waits for them, and re-layouts  2.78 us (2%)
    psum x1, waiting for transfers between devices, shards(): coeffs = lax.psum(partial_value, 'wave')  54.8 us
    reduce_scatter x1, waiting for transfers between devices, shards(): summed = lax.psum_scatter(terms, 'atom', scatter_dimension=1, tiled=True)  34.6 us
    dot_general x1, matrix products, shards(): jnp.einsum('ws,dsb->dwb', slab, inner, precision=lax.Precision.HIGHEST)  2.61 us
  transfers between devices with their start and end apart: 2, of which 2 were waited for; matrix products, arithmetic and copies ran while one was open for 1% of the time, Pallas kernels for 0%

commit v1 on v0

v1 whole, which is shorter than its diff:
```python
import functools

import jax
import jax.numpy as jnp
from jax import lax
from jax.experimental import pallas as pl
from jax.experimental.pallas import tpu as pltpu
from jax.sharding import PartitionSpec as P

MESH = pl.DeviceIdType.MESH


def general_shards(slab, orbitals, sphere_ops, wave_terms):
    partial_value = jnp.dot(
        slab.T, orbitals, preferred_element_type=jnp.float32, precision=lax.Precision.HIGHEST
    )
    coeffs = lax.psum(partial_value, "wave")
    atoms_here = sphere_ops.shape[1]
    width = sphere_ops.shape[2]
    blocks = coeffs.reshape(atoms_here, width, coeffs.shape[1])
    inner = jnp.einsum("dalm,amb->dalb", sphere_ops, blocks, precision=lax.Precision.HIGHEST)
    inner = inner.reshape(inner.shape[0], atoms_here * width, coeffs.shape[1])
    own_rows = orbitals.shape[0] // lax.axis_size("atom")
    first_row = lax.axis_index("atom") * own_rows
    own_orbitals = lax.dynamic_slice_in_dim(orbitals, first_row, own_rows, 0)
    own_factors = lax.dynamic_slice_in_dim(wave_terms, first_row, own_rows, 1)
    local_part = own_factors[:, :, None] * own_orbitals[None]
    terms = jnp.einsum("ws,dsb->dwb", slab, inner, precision=lax.Precision.HIGHEST)
    summed = lax.psum_scatter(terms, "atom", scatter_dimension=1, tiled=True)
    return summed + local_part


def halves(value):
    high = value.astype(jnp.bfloat16)
    low = (value - high.astype(jnp.float32)).astype(jnp.bfloat16)
    return high, low


def product(left, right, dims=((1,), (0,))):
    dot = functools.partial(
        lax.dot_general, dimension_numbers=(dims, ((), ())), preferred_element_type=jnp.float32
    )
    return dot(left[0], right[0]) + (dot(left[0], right[1]) + dot(left[1], right[0]))


def kernel(nw, na, slab_ref, orb_ref, ops_ref, wt_ref, out_ref,
           ops_own, ops_got, ops_all, slab_got, part, sums_got, piece, coeffs, left_side,
           ops_z, slab_z, rs, co_z, ops_p, co_p, ops_f, co_f):
    w = lax.axis_index("wave")
    a = lax.axis_index("atom")
    sister = w + 1 - 2 * lax.rem(w, 2)
    chips = nw // 2
    directions, atoms, width, _ = ops_ref.shape
    rows = slab_ref.shape[0] // na
    functions = slab_ref.shape[1]
    share = functions // nw
    ops_share = directions * width // nw

    def plane(k):
        return lax.rem(w + k, nw)

    def line(k):
        return lax.rem(a + k, na)

    barrier = pltpu.get_barrier_semaphore()
    for k in range(1, nw):
        pl.semaphore_signal(barrier, inc=1, device_id=(plane(k), a), device_id_type=MESH)
    for k in range(1, na):
        pl.semaphore_signal(barrier, inc=1, device_id=(w, line(k)), device_id_type=MESH)

    for d in range(directions):
        for i in range(atoms):
            ops_own[pl.ds(d * width, width), pl.ds(i * width, width)] = ops_ref[d, i]

    pl.semaphore_wait(barrier, nw - 1 + na - 1)

    def send(src, dst, sems, slot, device):
        copy = pltpu.make_async_remote_copy(
            src_ref=src, dst_ref=dst, send_sem=sems.at[0, slot], recv_sem=sems.at[1, slot],
            device_id=device, device_id_type=MESH,
        )
        copy.start()
        return copy

    own_ops_rows = pl.ds(pl.multiple_of(w * ops_share, 8), ops_share)
    ops_line = [
        send(ops_own.at[own_ops_rows], ops_got.at[na - 1 - k], ops_z, k, (w, line(k))) for k in range(1, na)
    ]
    slab_line = [
        send(slab_ref.at[pl.ds(pl.multiple_of(line(k) * rows, 8), rows)], slab_got.at[na - 1 - k],
             slab_z, k, (w, line(k)))
        for k in range(1, na)
    ]

    total = product(halves(slab_ref[...]), halves(orb_ref[...]), ((0,), (0,)))
    part[...] = total.reshape(part.shape)
    pieces = [
        send(part.at[plane(k)], sums_got.at[k - 1], rs, k, (plane(k), a)) for k in range(1, nw)
    ]

    own_rows = pl.ds(pl.multiple_of(a * rows, 128), rows)
    own_orbitals = orb_ref[own_rows, :]
    on_diagonal = lax.broadcasted_iota(jnp.int32, (rows, rows), 0) == lax.broadcasted_iota(
        jnp.int32, (rows, rows), 1)
    for d in range(directions):
        factors = jnp.broadcast_to(wt_ref[pl.ds(d, 1), own_rows], (rows, rows))
        column = jnp.sum(jnp.where(on_diagonal, factors, 0.0), axis=1, keepdims=True)
        out_ref[d] = column * own_orbitals

    mine = part[w]
    for k in range(1, nw):
        pieces[k - 1].wait_recv()
        mine = mine + sums_got[k - 1]
    piece[na - 1] = mine
    co_line = [
        send(piece.at[na - 1], piece.at[na - 1 - k], co_z, k, (w, line(k))) for k in range(1, na)
    ]

    for copy in ops_line:
        copy.wait_recv()
    ops_plane = [
        send(ops_got, ops_all.at[w], ops_p, q, (lax.rem(w + 2 * q, nw), a)) for q in range(1, chips)
    ]
    ops_plane.append(send(ops_got, ops_all.at[w], ops_p, 0, (sister, a)))
    ops_all[w] = ops_got[...]

    for copy in co_line:
        copy.wait_recv()
    co_plane = [
        send(piece, coeffs.at[w], co_p, q, (lax.rem(w + 2 * q, nw), a)) for q in range(1, chips)
    ]
    co_plane.append(send(piece, coeffs.at[w], co_p, 0, (sister, a)))
    coeffs[w] = piece[...]

    def forward(arrived, buffer, sems):
        copies = []
        for q in range(1, chips):
            arrived[q - 1].wait_recv()
            source = lax.rem(w - 2 * q + nw, nw)
            copies.append(send(buffer.at[source], buffer.at[source], sems, q, (sister, a)))
        return copies

    ops_sister = forward(ops_plane, ops_all, ops_f)
    co_sister = forward(co_plane, coeffs, co_f)

    ops_plane[-1].wait_recv()
    for copy in ops_sister:
        copy.wait_recv()
    for copy in slab_line:
        copy.wait_recv()
    lane_atom = lax.broadcasted_iota(jnp.int32, (width, functions), 1) // width
    for s in range(na):
        if s == na - 1:
            stacked = ops_own[...]
            own_slab = slab_ref[own_rows, :]
        else:
            stacked = ops_all[:, s].reshape(directions * width, functions)
            own_slab = slab_got[s]
        slab_halves = halves(own_slab)
        for d in range(directions):
            rows_d = stacked[d * width:(d + 1) * width]
            block = jnp.concatenate(
                [jnp.where(lane_atom == i, rows_d, 0.0) for i in range(atoms)], axis=0)
            left_side[pl.ds(d * rows, rows), pl.ds(s * functions, functions)] = product(
                slab_halves, halves(block))

    co_plane[-1].wait_recv()
    for copy in co_sister:
        copy.wait_recv()
    gathered = jnp.concatenate(
        [coeffs[:, s].reshape(functions, orb_ref.shape[1]) for s in range(na)], axis=0)
    coeff_halves = halves(gathered)
    for d in range(directions):
        out_ref[d] += product(halves(left_side[pl.ds(d * rows, rows), :]), coeff_halves)

    for copy in ops_line + slab_line + pieces + co_line + ops_plane + co_plane + ops_sister + co_sister:
        copy.wait_send()


def kernel_shards(nw, na, slab, orbitals, sphere_ops, wave_terms):
    directions, atoms, width, _ = sphere_ops.shape
    waves, functions = slab.shape
    columns = orbitals.shape[1]
    rows = waves // na
    share = functions // nw
    ops_share = directions * width // nw
    f32 = jnp.float32

    def dma(count):
        return pltpu.SemaphoreType.DMA((2, count))

    vmem = pl.BlockSpec(memory_space=pltpu.VMEM)
    return pl.pallas_call(
        functools.partial(kernel, nw, na),
        out_shape=jax.ShapeDtypeStruct((directions, rows, columns), f32),
        in_specs=[vmem] * 4,
        out_specs=vmem,
        scratch_shapes=[
            pltpu.VMEM((directions * width, functions), f32),
            pltpu.VMEM((na - 1, ops_share, functions), f32),
            pltpu.VMEM((nw, na - 1, ops_share, functions), f32),
            pltpu.VMEM((na - 1, rows, functions), f32),
            pltpu.VMEM((nw, share, columns), f32),
            pltpu.VMEM((nw - 1, share, columns), f32),
            pltpu.VMEM((na, share, columns), f32),
            pltpu.VMEM((nw, na, share, columns), f32),
            pltpu.VMEM((directions * rows, na * functions), f32),
            dma(na), dma(na), dma(nw), dma(na),
            dma(nw // 2), dma(nw // 2), dma(nw // 2), dma(nw // 2),
        ],
        compiler_params=pltpu.CompilerParams(
            collective_id=0, has_side_effects=True, vmem_limit_bytes=32 * 1024 * 1024,
        ),
        cost_estimate=pl.CostEstimate(
            flops=6 * waves * functions * columns * (1 + directions), bytes_accessed=2 * 1024 * 1024,
            transcendentals=0),
    )(slab, orbitals, sphere_ops, wave_terms)


def shards(nw, na, slab, orbitals, sphere_ops, wave_terms):
    directions, atoms, width, _ = sphere_ops.shape
    waves, functions = slab.shape
    fits = (
        nw % 2 == 0 and nw > 2 and na > 1
        and functions % (8 * nw) == 0 and (directions * width) % (8 * nw) == 0
        and atoms * width == functions and functions % 128 == 0
        and waves % (128 * na) == 0 and orbitals.shape[1] % 128 == 0
    )
    if fits:
        return kernel_shards(nw, na, slab, orbitals, sphere_ops, wave_terms)
    return general_shards(slab, orbitals, sphere_ops, wave_terms)


def solution(mesh):
    return jax.shard_map(
        functools.partial(shards, mesh.shape["wave"], mesh.shape["atom"]),
        mesh=mesh,
        in_specs=(P("wave", "atom"), P("wave", None), P(None, "atom", None, None), P(None, "wave")),
        out_specs=P(None, ("wave", "atom"), None),
        check_vma=False,
    )
```

time: 114 us -> 25.6 us (0.22)
  waiting for transfers between devices: 89.4 us -> 0 us
  Pallas kernels: 0 us -> 21 us
  between operations: 13.4 us -> 0.01 us
  matrix products: 6.27 us -> 0 us
  local copies, waits for them, and re-layouts: 2.78 us -> 4.36 us
    psum x1 -> x0, waiting for transfers between devices: 54.8 us -> none  [shards(): coeffs = lax.psum(partial_value, 'wave')]
    reduce_scatter x1 -> x0, waiting for transfers between devices: 34.6 us -> none  [shards(): summed = lax.psum_scatter(terms, 'atom', scatter_dimension=1, tiled=True)]
    pallas_call x0 -> x1, Pallas kernels: none -> 21 us  [kernel_shards(): pl.pallas_call(functools.partial(kernel, nw, na), out_shape=jax.ShapeDtyp...]
    dot_general x3 -> x0, matrix products: 6.27 us -> none  [the longest x1 2.61 us: shards(): jnp.einsum('ws,dsb->dwb', slab, inner, precision=lax.Precision.HIGHEST)]
    unnamed x4 -> x9, local copies, waits for them, and re-layouts: 1.04 us -> 4.36 us
  transfers between devices with their start and end apart: 2 -> 0, of which waited for: 2 -> 0; matrix products, arithmetic and copies ran while one was open for 1% -> 0% of each run, Pallas kernels for 0% -> 0%
where the time goes in v1:
time: 25.6 us; the launch traced here: 25.4 us
  Pallas kernels  21 us (82%)
  local copies, waits for them, and re-layouts  4.36 us (17%)
    pallas_call x1, Pallas kernels, kernel_shards(): pl.pallas_call(functools.partial(kernel, nw, na), out_shape=jax.ShapeDtyp...  21 us
    unnamed x9, local copies, waits for them, and re-layouts  4.36 us

profile of v1, /device:TPU:1, one launch (start us, length us, event | category | flops | bytes accessed | tf_op | source)
XLA Modules:
  0.0 25.4 jit_solution(6502478666911568633)
XLA Ops:
  0.0 0.0 copy-start
  0.0 1.0 %copy-done = f32[512,256]{1,0:T(8,128)S(1)} copy-done((f32[512,256]{1,0:T(8,128)S(1)}, f32[512,256]{1,0:T(8,128)}, u32[]{:S(2)}) %copy-start) | copy-done | bytes 524312
  1.0 0.0 copy-start.1
  1.0 0.9 %copy-done.1 = f32[512,128]{1,0:T(8,128)S(1)} copy-done((f32[512,128]{1,0:T(8,128)S(1)}, f32[512,128]{1,0:T(8,128)}, u32[]{:S(2)}) %copy-start.1) | copy-done | bytes 262168
  2.0 0.0 copy-start.2
  2.0 0.9 %copy-done.2 = f32[3,2,64,64]{3,2,1,0:T(8,128)S(1)} copy-done((f32[3,2,64,64]{3,2,1,0:T(8,128)S(1)}, f32[3,2,64,64]{3,2,1,0:T(8,128)}, u32[]{:S(2)}) %copy-start.2) | copy-done | bytes 98328
  2.9 0.0 copy-start.3
  2.9 0.7 %copy-done.3 = f32[3,512]{1,0:T(4,128)S(1)} copy-done((f32[3,512]{1,0:T(4,128)S(1)}, f32[3,512]{1,0:T(4,128)}, u32[]{:S(2)}) %copy-start.3) | copy-done | bytes 6168
  3.6 21.0 %shard_map.46 = f32[3,128,256]{2,1,0:T(8,128)S(1)} custom-call(f32[512,128]{1,0:T(8,128)S(1)} %copy-done.1, f32[512,256]{1,0:T(8,128)S(1)} %copy-done, f32[3,2,64,64]{3,2,1,0:T(8,128)S(1)} %copy-done.2, f32[3,512]{1,0:T(4,128)S(1)} %copy-done.3), custom_call_target="tpu_custom_call" | custom-call | flops 402653184 | bytes 2097152 | tf_op jit(solution)/shard_map/pallas_call | solution.py:193
  24.6 0.7 %copy.6 = f32[3,128,256]{2,1,0:T(8,128)} copy(f32[3,128,256]{2,1,0:T(8,128)S(1)} %shard_map.46) | data formatting | bytes 786432
Async XLA Ops:
  0.0 1.0 %copy-start = (f32[512,256]{1,0:T(8,128)S(1)}, f32[512,256]{1,0:T(8,128)}, u32[]{:S(2)}) copy-start(f32[512,256]{1,0:T(8,128)} %orb_ref.1) | copy-start | bytes 1572868
  1.0 0.9 %copy-start.1 = (f32[512,128]{1,0:T(8,128)S(1)}, f32[512,128]{1,0:T(8,128)}, u32[]{:S(2)}) copy-start(f32[512,128]{1,0:T(8,128)} %slab_ref.1) | copy-start | bytes 786436
  2.0 0.9 %copy-start.2 = (f32[3,2,64,64]{3,2,1,0:T(8,128)S(1)}, f32[3,2,64,64]{3,2,1,0:T(8,128)}, u32[]{:S(2)}) copy-start(f32[3,2,64,64]{3,2,1,0:T(8,128)} %ops_ref.1) | copy-start | bytes 294916
  2.9 0.7 %copy-start.3 = (f32[3,512]{1,0:T(4,128)S(1)}, f32[3,512]{1,0:T(4,128)}, u32[]{:S(2)}) copy-start(f32[3,512]{1,0:T(4,128)} %wt_ref.1) | copy-start | bytes 18436

commit v2 on v1

v2 whole, which is shorter than its diff:
```python
import functools

import jax
import jax.numpy as jnp
from jax import lax
from jax.experimental import pallas as pl
from jax.experimental.pallas import tpu as pltpu
from jax.sharding import PartitionSpec as P

MESH = pl.DeviceIdType.MESH


def general_shards(slab, orbitals, sphere_ops, wave_terms):
    partial_value = jnp.dot(
        slab.T, orbitals, preferred_element_type=jnp.float32, precision=lax.Precision.HIGHEST
    )
    coeffs = lax.psum(partial_value, "wave")
    atoms_here = sphere_ops.shape[1]
    width = sphere_ops.shape[2]
    blocks = coeffs.reshape(atoms_here, width, coeffs.shape[1])
    inner = jnp.einsum("dalm,amb->dalb", sphere_ops, blocks, precision=lax.Precision.HIGHEST)
    inner = inner.reshape(inner.shape[0], atoms_here * width, coeffs.shape[1])
    own_rows = orbitals.shape[0] // lax.axis_size("atom")
    first_row = lax.axis_index("atom") * own_rows
    own_orbitals = lax.dynamic_slice_in_dim(orbitals, first_row, own_rows, 0)
    own_factors = lax.dynamic_slice_in_dim(wave_terms, first_row, own_rows, 1)
    local_part = own_factors[:, :, None] * own_orbitals[None]
    terms = jnp.einsum("ws,dsb->dwb", slab, inner, precision=lax.Precision.HIGHEST)
    summed = lax.psum_scatter(terms, "atom", scatter_dimension=1, tiled=True)
    return summed + local_part


def halves(value):
    high = value.astype(jnp.bfloat16)
    low = (value - high.astype(jnp.float32)).astype(jnp.bfloat16)
    return high, low


def product(left, right, dims=((1,), (0,))):
    dot = functools.partial(
        lax.dot_general, dimension_numbers=(dims, ((), ())), preferred_element_type=jnp.float32
    )
    return dot(left[0], right[0]) + (dot(left[0], right[1]) + dot(left[1], right[0]))


def kernel(nw, na, slab_hbm, orb_hbm, ops_hbm, wt_hbm, out_ref,
           slab_ref, orb_ref, ops_ref, wt_ref, ops_own, ops_got, ops_all, slab_got, part, sums_got, piece,
           coeffs, left_high, left_low, loads, ops_z, slab_z, rs, co_z, ops_p, ops_f, own_p, own_f, co_p, co_f):
    w = lax.axis_index("wave")
    a = lax.axis_index("atom")
    sister = w + 1 - 2 * lax.rem(w, 2)
    chips = nw // 2
    directions, atoms, width, _ = ops_ref.shape
    rows = slab_ref.shape[0] // na
    functions = slab_ref.shape[1]
    ops_share = directions * width // nw
    last = na - 1

    def plane(k):
        return lax.rem(w + k, nw)

    def line(k):
        return lax.rem(a + k, na)

    barrier = pltpu.get_barrier_semaphore()
    for k in range(1, na):
        pl.semaphore_signal(barrier, inc=1, device_id=(w, line(k)), device_id_type=MESH)
    for k in range(1, nw):
        pl.semaphore_signal(barrier, inc=1, device_id=(plane(k), a), device_id_type=MESH)

    local = [
        pltpu.make_async_copy(src, dst, loads.at[n])
        for n, (src, dst) in enumerate(
            ((ops_hbm, ops_ref), (slab_hbm, slab_ref), (orb_hbm, orb_ref), (wt_hbm, wt_ref)))
    ]
    for copy in local:
        copy.start()

    local[0].wait()
    for d in range(directions):
        for i in range(atoms):
            ops_own[pl.ds(d * width, width), pl.ds(i * width, width)] = ops_ref[d, i]

    started = []

    def send(src, dst, sems, slot, device):
        copy = pltpu.make_async_remote_copy(
            src_ref=src, dst_ref=dst, send_sem=sems.at[0, slot], recv_sem=sems.at[1, slot],
            device_id=device, device_id_type=MESH,
        )
        copy.start()
        started.append(copy)
        return copy

    def spread(src, dst, sems):
        copies = [send(src, dst, sems, q, (plane(2 * q), a)) for q in range(1, chips)]
        return copies + [send(src, dst, sems, 0, (sister, a))]

    def forward(arrived, block_of, sems):
        copies = []
        for q in range(1, chips):
            arrived[q - 1].wait_recv()
            block = block_of(lax.rem(w - 2 * q + nw, nw))
            copies.append(send(block, block, sems, q, (sister, a)))
        return copies

    pl.semaphore_wait(barrier, nw - 1 + na - 1)

    own_ops_rows = pl.ds(pl.multiple_of(w * ops_share, 8), ops_share)
    ops_line = [
        send(ops_own.at[own_ops_rows], ops_got.at[last - k], ops_z, k, (w, line(k))) for k in range(1, na)
    ]
    slab_line = [
        send(slab_hbm.at[pl.ds(pl.multiple_of(line(k) * rows, 8), rows)], slab_got.at[last - k],
             slab_z, k, (w, line(k)))
        for k in range(1, na)
    ]

    local[1].wait()
    local[2].wait()
    total = product(halves(slab_ref[...]), halves(orb_ref[...]), ((0,), (0,)))
    part[...] = total.reshape(part.shape)
    pieces = [
        send(part.at[plane(k)], sums_got.at[k - 1], rs, k, (plane(k), a)) for k in range(1, nw)
    ]

    own_rows = pl.ds(pl.multiple_of(a * rows, 128), rows)
    own_orbitals = orb_ref[own_rows, :]
    on_diagonal = lax.broadcasted_iota(jnp.int32, (rows, rows), 0) == lax.broadcasted_iota(
        jnp.int32, (rows, rows), 1)
    local[3].wait()
    for d in range(directions):
        factors = jnp.broadcast_to(wt_ref[pl.ds(d, 1), own_rows], (rows, rows))
        column = jnp.sum(jnp.where(on_diagonal, factors, 0.0), axis=1, keepdims=True)
        out_ref[d] = column * own_orbitals

    lane_atom = lax.broadcasted_iota(jnp.int32, (width, functions), 1) // width

    def apply_blocks(s, own_slab, stacked):
        blocks = [
            jnp.concatenate([
                jnp.where(lane_atom == i, stacked[d * width:(d + 1) * width], 0.0) for i in range(atoms)
            ], axis=0)
            for d in range(directions)
        ]
        high, low = halves(product(halves(own_slab), halves(jnp.concatenate(blocks, axis=1))))
        for d in range(directions):
            at = (pl.ds(d * rows, rows), pl.ds(s * functions, functions))
            left_high[at] = high[:, d * functions:(d + 1) * functions]
            left_low[at] = low[:, d * functions:(d + 1) * functions]

    apply_blocks(last, slab_ref[own_rows, :], ops_own[...])

    for copy in ops_line:
        copy.wait_recv()
    ops_plane = spread(ops_got, ops_all.at[w], ops_p)
    ops_all[w] = ops_got[...]

    mine = part[w]
    for k in range(1, nw):
        pieces[k - 1].wait_recv()
        mine = mine + sums_got[k - 1]
    piece[last] = mine
    co_line = [send(piece.at[last], piece.at[last - k], co_z, k, (w, line(k))) for k in range(1, na)]
    own_plane = spread(piece.at[last], coeffs.at[w, last], own_p)
    ops_sister = forward(ops_plane, lambda source: ops_all.at[source], ops_f)
    for copy in co_line:
        copy.wait_recv()
    others = pl.ds(0, last)
    co_plane = spread(piece.at[others], coeffs.at[w, others], co_p)
    coeffs[w] = piece[...]
    own_sister = forward(own_plane, lambda source: coeffs.at[source, last], own_f)

    ops_plane[-1].wait_recv()
    for copy in ops_sister:
        copy.wait_recv()
    for k in range(1, na):
        s = last - k
        slab_line[k - 1].wait_recv()
        apply_blocks(s, slab_got[s], ops_all[:, s].reshape(directions * width, functions))

    co_sister = forward(co_plane, lambda source: coeffs.at[source, others], co_f)
    for copy in [own_plane[-1], co_plane[-1]] + own_sister + co_sister:
        copy.wait_recv()
    gathered = jnp.concatenate(
        [coeffs[:, s].reshape(functions, orb_ref.shape[1]) for s in range(na)], axis=0)
    coeff_halves = halves(gathered)
    for d in range(directions):
        at = pl.ds(d * rows, rows)
        out_ref[d] += product((left_high[at, :], left_low[at, :]), coeff_halves)

    for copy in started:
        copy.wait_send()


def kernel_shards(nw, na, slab, orbitals, sphere_ops, wave_terms):
    directions, atoms, width, _ = sphere_ops.shape
    waves, functions = slab.shape
    columns = orbitals.shape[1]
    rows = waves // na
    share = functions // nw
    ops_share = directions * width // nw
    f32 = jnp.float32

    def dma(count):
        return pltpu.SemaphoreType.DMA((2, count))

    return pl.pallas_call(
        functools.partial(kernel, nw, na),
        out_shape=jax.ShapeDtypeStruct((directions, rows, columns), f32),
        in_specs=[pl.BlockSpec(memory_space=pltpu.HBM)] * 4,
        out_specs=pl.BlockSpec(memory_space=pltpu.VMEM),
        scratch_shapes=[
            pltpu.VMEM(slab.shape, f32),
            pltpu.VMEM(orbitals.shape, f32),
            pltpu.VMEM(sphere_ops.shape, f32),
            pltpu.VMEM(wave_terms.shape, f32),
            pltpu.VMEM((directions * width, functions), f32),
            pltpu.VMEM((na - 1, ops_share, functions), f32),
            pltpu.VMEM((nw, na - 1, ops_share, functions), f32),
            pltpu.VMEM((na - 1, rows, functions), f32),
            pltpu.VMEM((nw, share, columns), f32),
            pltpu.VMEM((nw - 1, share, columns), f32),
            pltpu.VMEM((na, share, columns), f32),
            pltpu.VMEM((nw, na, share, columns), f32),
            pltpu.VMEM((directions * rows, na * functions), jnp.bfloat16),
            pltpu.VMEM((directions * rows, na * functions), jnp.bfloat16),
            pltpu.SemaphoreType.DMA((4,)),
            dma(na), dma(na), dma(nw), dma(na),
            dma(nw // 2), dma(nw // 2), dma(nw // 2), dma(nw // 2), dma(nw // 2), dma(nw // 2),
        ],
        compiler_params=pltpu.CompilerParams(
            collective_id=0, has_side_effects=True, vmem_limit_bytes=60 * 1024 * 1024,
        ),
        cost_estimate=pl.CostEstimate(
            flops=6 * waves * functions * columns * (1 + directions), bytes_accessed=2 * 1024 * 1024,
            transcendentals=0),
    )(slab, orbitals, sphere_ops, wave_terms)


def shards(nw, na, slab, orbitals, sphere_ops, wave_terms):
    directions, atoms, width, _ = sphere_ops.shape
    waves, functions = slab.shape
    fits = (
        nw % 2 == 0 and nw > 2 and na > 1
        and functions % (8 * nw) == 0 and (directions * width) % (8 * nw) == 0
        and atoms * width == functions and functions % 128 == 0
        and waves % (128 * na) == 0 and orbitals.shape[1] % 128 == 0
    )
    if fits:
        return kernel_shards(nw, na, slab, orbitals, sphere_ops, wave_terms)
    return general_shards(slab, orbitals, sphere_ops, wave_terms)


def solution(mesh):
    return jax.shard_map(
        functools.partial(shards, mesh.shape["wave"], mesh.shape["atom"]),
        mesh=mesh,
        in_specs=(P("wave", "atom"), P("wave", None), P(None, "atom", None, None), P(None, "wave")),
        out_specs=P(None, ("wave", "atom"), None),
        check_vma=False,
    )
```

time: 25.6 us -> 23.6 us (0.922)
  local copies, waits for them, and re-layouts: 4.36 us -> 1.77 us
  Pallas kernels: 21 us -> 21.7 us
    unnamed x9 -> x1, local copies, waits for them, and re-layouts: 4.36 us -> 1.77 us
    pallas_call x1, Pallas kernels: 21 us -> 21.7 us  [kernel_shards(): pl.pallas_call(functools.partial(kernel, nw, na), out_shape=jax.ShapeDtyp...]
where the time goes in v2:
time: 23.6 us; the launch traced here: 23.4 us
  Pallas kernels  21.7 us (92%)
  local copies, waits for them, and re-layouts  1.77 us (7%)
    pallas_call x1, Pallas kernels, kernel_shards(): pl.pallas_call(functools.partial(kernel, nw, na), out_shape=jax.ShapeDtyp...  21.7 us
    unnamed x1, local copies, waits for them, and re-layouts  1.77 us

profile of v2, /device:TPU:1, one launch (start us, length us, event | category | flops | bytes accessed | tf_op | source)
XLA Modules:
  0.0 23.4 jit_solution(1217260715802614161)
XLA Ops:
  0.0 21.7 %shard_map.46 = f32[3,128,256]{2,1,0:T(8,128)} custom-call(f32[512,128]{1,0:T(8,128)} %slab_hbm.1, f32[512,256]{1,0:T(8,128)} %orb_hbm.1, f32[3,2,64,64]{3,2,1,0:T(8,128)} %ops_hbm.1, f32[3,512]{1,0:T(4,128)} %wt_hbm.1), custom_call_target="tpu_custom_call" | custom-call | flops 402653184 | bytes 2097152 | tf_op jit(solution)/shard_map/pallas_call | solution.py:208
  21.7 1.8 %copy.6 = f32[3,128,256]{2,1,0:T(8,128)} copy(f32[3,128,256]{2,1,0:T(8,128)} %shard_map.46) | data formatting | bytes 786432

commit v3 on v2

--- a/solution.py
+++ b/solution.py
@@ -104,25 +104,10 @@
             copies.append(send(block, block, sems, q, (sister, a)))
         return copies
 
-    pl.semaphore_wait(barrier, nw - 1 + na - 1)
-
-    own_ops_rows = pl.ds(pl.multiple_of(w * ops_share, 8), ops_share)
-    ops_line = [
-        send(ops_own.at[own_ops_rows], ops_got.at[last - k], ops_z, k, (w, line(k))) for k in range(1, na)
-    ]
-    slab_line = [
-        send(slab_hbm.at[pl.ds(pl.multiple_of(line(k) * rows, 8), rows)], slab_got.at[last - k],
-             slab_z, k, (w, line(k)))
-        for k in range(1, na)
-    ]
-
     local[1].wait()
     local[2].wait()
     total = product(halves(slab_ref[...]), halves(orb_ref[...]), ((0,), (0,)))
     part[...] = total.reshape(part.shape)
-    pieces = [
-        send(part.at[plane(k)], sums_got.at[k - 1], rs, k, (plane(k), a)) for k in range(1, nw)
-    ]
 
     own_rows = pl.ds(pl.multiple_of(a * rows, 128), rows)
     own_orbitals = orb_ref[own_rows, :]
@@ -145,16 +130,28 @@
         ]
         high, low = halves(product(halves(own_slab), halves(jnp.concatenate(blocks, axis=1))))
         for d in range(directions):
-            at = (pl.ds(d * rows, rows), pl.ds(s * functions, functions))
-            left_high[at] = high[:, d * functions:(d + 1) * functions]
-            left_low[at] = low[:, d * functions:(d + 1) * functions]
+            at = pl.ds(d * rows, rows)
+            left_high[s, at] = high[:, d * functions:(d + 1) * functions]
+            left_low[s, at] = low[:, d * functions:(d + 1) * functions]
 
     apply_blocks(last, slab_ref[own_rows, :], ops_own[...])
 
-    for copy in ops_line:
-        copy.wait_recv()
-    ops_plane = spread(ops_got, ops_all.at[w], ops_p)
-    ops_all[w] = ops_got[...]
+    pl.semaphore_wait(barrier, nw - 1 + na - 1)
+
+    pieces = [
+        send(part.at[plane(k)], sums_got.at[k - 1], rs, k, (plane(k), a)) for k in range(1, nw)
+    ]
+
+    own_ops_rows = pl.ds(pl.multiple_of(w * ops_share, 8), ops_share)
+    ops_line = [
+        send(ops_own.at[own_ops_rows], ops_got.at[last - k], ops_z, k, (w, line(k))) for k in range(1, na)
+    ]
+    slab_line = [
+        send(slab_hbm.at[pl.ds(pl.multiple_of(line(k) * rows, 8), rows)], slab_got.at[last - k],
+             slab_z, k, (w, line(k)))
+        for k in range(1, na)
+    ]
+
 
     mine = part[w]
     for k in range(1, nw):
@@ -163,11 +160,22 @@
     piece[last] = mine
     co_line = [send(piece.at[last], piece.at[last - k], co_z, k, (w, line(k))) for k in range(1, na)]
     own_plane = spread(piece.at[last], coeffs.at[w, last], own_p)
+
+    for copy in ops_line:
+        copy.wait_recv()
+    ops_plane = spread(ops_got, ops_all.at[w], ops_p)
+    ops_all[w] = ops_got[...]
     ops_sister = forward(ops_plane, lambda source: ops_all.at[source], ops_f)
-    for copy in co_line:
-        copy.wait_recv()
-    others = pl.ds(0, last)
-    co_plane = spread(piece.at[others], coeffs.at[w, others], co_p)
+    upper = (2 * a) // na
+    steps = [upper * (i + 1) + (1 - upper) * (last - i) for i in range(last)]
+    co_plane = []
+    for i, k in enumerate(steps):
+        s = last - k
+        pltpu.make_async_remote_copy(
+            src_ref=piece.at[last], dst_ref=piece.at[s], send_sem=co_z.at[0, k], recv_sem=co_z.at[1, k],
+            device_id=(w, line(1)), device_id_type=MESH,
+        ).wait_recv()
+        co_plane.append(spread(piece.at[s], coeffs.at[w, s], co_p.at[i]))
     coeffs[w] = piece[...]
     own_sister = forward(own_plane, lambda source: coeffs.at[source, last], own_f)
 
@@ -179,15 +187,21 @@
         slab_line[k - 1].wait_recv()
         apply_blocks(s, slab_got[s], ops_all[:, s].reshape(directions * width, functions))
 
-    co_sister = forward(co_plane, lambda source: coeffs.at[source, others], co_f)
-    for copy in [own_plane[-1], co_plane[-1]] + own_sister + co_sister:
-        copy.wait_recv()
-    gathered = jnp.concatenate(
-        [coeffs[:, s].reshape(functions, orb_ref.shape[1]) for s in range(na)], axis=0)
-    coeff_halves = halves(gathered)
-    for d in range(directions):
-        at = pl.ds(d * rows, rows)
-        out_ref[d] += product((left_high[at, :], left_low[at, :]), coeff_halves)
+    def add_slot(s, waits):
+        for copy in waits:
+            copy.wait_recv()
+        coeff_halves = halves(coeffs[:, s].reshape(functions, orb_ref.shape[1]))
+        for d in range(directions):
+            at = pl.ds(d * rows, rows)
+            out_ref[d] += product((left_high[s, at], left_low[s, at]), coeff_halves)
+
+    add_slot(last, [own_plane[-1]] + own_sister)
+    co_sister = [
+        forward(co_plane[i], lambda source, s=last - k: coeffs.at[source, s], co_f.at[i])
+        for i, k in enumerate(steps)
+    ]
+    for i, k in enumerate(steps):
+        add_slot(last - k, [co_plane[i][-1]] + co_sister[i])
 
     for copy in started:
         copy.wait_send()
@@ -223,11 +237,12 @@
             pltpu.VMEM((nw - 1, share, columns), f32),
             pltpu.VMEM((na, share, columns), f32),
             pltpu.VMEM((nw, na, share, columns), f32),
-            pltpu.VMEM((directions * rows, na * functions), jnp.bfloat16),
-            pltpu.VMEM((directions * rows, na * functions), jnp.bfloat16),
+            pltpu.VMEM((na, directions * rows, functions), jnp.bfloat16),
+            pltpu.VMEM((na, directions * rows, functions), jnp.bfloat16),
             pltpu.SemaphoreType.DMA((4,)),
             dma(na), dma(na), dma(nw), dma(na),
-            dma(nw // 2), dma(nw // 2), dma(nw // 2), dma(nw // 2), dma(nw // 2), dma(nw // 2),
+            dma(nw // 2), dma(nw // 2), dma(nw // 2), dma(nw // 2),
+            pltpu.SemaphoreType.DMA((na - 1, 2, nw // 2)), pltpu.SemaphoreType.DMA((na - 1, 2, nw // 2)),
         ],
         compiler_params=pltpu.CompilerParams(
             collective_id=0, has_side_effects=True, vmem_limit_bytes=60 * 1024 * 1024,

time: 23.6 us -> 24.1 us (1.021)
  Pallas kernels: 21.7 us -> 22.1 us
    pallas_call x1, Pallas kernels: 21.7 us -> 22.1 us  [kernel_shards(): pl.pallas_call(functools.partial(kernel, nw, na), out_shape=jax.ShapeDtyp...]
where the time goes in v3:
time: 24.1 us; the launch traced here: 23.9 us
  Pallas kernels  22.1 us (92%)
  local copies, waits for them, and re-layouts  1.77 us (7%)
    pallas_call x1, Pallas kernels, kernel_shards(): pl.pallas_call(functools.partial(kernel, nw, na), out_shape=jax.ShapeDtyp...  22.1 us
    unnamed x1, local copies, waits for them, and re-layouts  1.77 us

profile of v3, /device:TPU:1, one launch (start us, length us, event | category | flops | bytes accessed | tf_op | source)
XLA Modules:
  0.0 23.9 jit_solution(15678569871569239128)
XLA Ops:
  0.0 22.1 %shard_map.46 = f32[3,128,256]{2,1,0:T(8,128)} custom-call(f32[512,128]{1,0:T(8,128)} %slab_hbm.1, f32[512,256]{1,0:T(8,128)} %orb_hbm.1, f32[3,2,64,64]{3,2,1,0:T(8,128)} %ops_hbm.1, f32[3,512]{1,0:T(4,128)} %wt_hbm.1), custom_call_target="tpu_custom_call" | custom-call | flops 402653184 | bytes 2097152 | tf_op jit(solution)/shard_map/pallas_call | solution.py:222
  22.1 1.8 %copy.6 = f32[3,128,256]{2,1,0:T(8,128)} copy(f32[3,128,256]{2,1,0:T(8,128)} %shard_map.46) | data formatting | bytes 786432

commit v4 on v3

--- a/solution.py
+++ b/solution.py
@@ -152,7 +152,6 @@
         for k in range(1, na)
     ]
 
-
     mine = part[w]
     for k in range(1, nw):
         pieces[k - 1].wait_recv()
@@ -165,7 +164,7 @@
         copy.wait_recv()
     ops_plane = spread(ops_got, ops_all.at[w], ops_p)
     ops_all[w] = ops_got[...]
-    ops_sister = forward(ops_plane, lambda source: ops_all.at[source], ops_f)
+
     upper = (2 * a) // na
     steps = [upper * (i + 1) + (1 - upper) * (last - i) for i in range(last)]
     co_plane = []
@@ -177,6 +176,7 @@
         ).wait_recv()
         co_plane.append(spread(piece.at[s], coeffs.at[w, s], co_p.at[i]))
     coeffs[w] = piece[...]
+    ops_sister = forward(ops_plane, lambda source: ops_all.at[source], ops_f)
     own_sister = forward(own_plane, lambda source: coeffs.at[source, last], own_f)
 
     ops_plane[-1].wait_recv()

time: 24.1 us -> 24.1 us (level)
  no operation moved by 1% of the time
where the time goes in v4:
time: 24.1 us; the launch traced here: 23.9 us
  Pallas kernels  22.1 us (92%)
  local copies, waits for them, and re-layouts  1.77 us (7%)
    pallas_call x1, Pallas kernels, kernel_shards(): pl.pallas_call(functools.partial(kernel, nw, na), out_shape=jax.ShapeDtyp...  22.1 us
    unnamed x1, local copies, waits for them, and re-layouts  1.77 us

profile of v4, /device:TPU:1, one launch (start us, length us, event | category | flops | bytes accessed | tf_op | source)
XLA Modules:
  0.0 23.9 jit_solution(1968567057620176206)
XLA Ops:
  0.0 22.1 %shard_map.46 = f32[3,128,256]{2,1,0:T(8,128)} custom-call(f32[512,128]{1,0:T(8,128)} %slab_hbm.1, f32[512,256]{1,0:T(8,128)} %orb_hbm.1, f32[3,2,64,64]{3,2,1,0:T(8,128)} %ops_hbm.1, f32[3,512]{1,0:T(4,128)} %wt_hbm.1), custom_call_target="tpu_custom_call" | custom-call | flops 402653184 | bytes 2097152 | tf_op jit(solution)/shard_map/pallas_call | solution.py:222
  22.1 1.8 %copy.6 = f32[3,128,256]{2,1,0:T(8,128)} copy(f32[3,128,256]{2,1,0:T(8,128)} %shard_map.46) | data formatting | bytes 786432

commit v5 on v4

--- a/solution.py
+++ b/solution.py
@@ -146,11 +146,16 @@
     ops_line = [
         send(ops_own.at[own_ops_rows], ops_got.at[last - k], ops_z, k, (w, line(k))) for k in range(1, na)
     ]
-    slab_line = [
-        send(slab_hbm.at[pl.ds(pl.multiple_of(line(k) * rows, 8), rows)], slab_got.at[last - k],
-             slab_z, k, (w, line(k)))
-        for k in range(1, na)
-    ]
+    half = rows // 2
+
+    def send_slab(h):
+        return [
+            send(slab_hbm.at[pl.ds(pl.multiple_of(line(k) * rows + h * half, 8), half)],
+                 slab_got.at[last - k, pl.ds(h * half, half)], slab_z, h * na + k, (w, line(k)))
+            for k in range(1, na)
+        ]
+
+    slab_line = send_slab(0)
 
     mine = part[w]
     for k in range(1, nw):
@@ -159,6 +164,7 @@
     piece[last] = mine
     co_line = [send(piece.at[last], piece.at[last - k], co_z, k, (w, line(k))) for k in range(1, na)]
     own_plane = spread(piece.at[last], coeffs.at[w, last], own_p)
+    slab_line += send_slab(1)
 
     for copy in ops_line:
         copy.wait_recv()
@@ -185,6 +191,7 @@
     for k in range(1, na):
         s = last - k
         slab_line[k - 1].wait_recv()
+        slab_line[last + k - 1].wait_recv()
         apply_blocks(s, slab_got[s], ops_all[:, s].reshape(directions * width, functions))
 
     def add_slot(s, waits):
@@ -240,7 +247,7 @@
             pltpu.VMEM((na, directions * rows, functions), jnp.bfloat16),
             pltpu.VMEM((na, directions * rows, functions), jnp.bfloat16),
             pltpu.SemaphoreType.DMA((4,)),
-            dma(na), dma(na), dma(nw), dma(na),
+            dma(na), dma(2 * na), dma(nw), dma(na),
             dma(nw // 2), dma(nw // 2), dma(nw // 2), dma(nw // 2),
             pltpu.SemaphoreType.DMA((na - 1, 2, nw // 2)), pltpu.SemaphoreType.DMA((na - 1, 2, nw // 2)),
         ],

time: 24.1 us -> 21.7 us (0.900)
  Pallas kernels: 22.1 us -> 19.6 us
    pallas_call x1, Pallas kernels: 22.1 us -> 19.6 us  [kernel_shards(): pl.pallas_call(functools.partial(kernel, nw, na), out_shape=jax.ShapeDtyp...]
where the time goes in v5:
time: 21.7 us; the launch traced here: 21.4 us
  Pallas kernels  19.6 us (90%)
  local copies, waits for them, and re-layouts  1.77 us (8%)
    pallas_call x1, Pallas kernels, kernel_shards(): pl.pallas_call(functools.partial(kernel, nw, na), out_shape=jax.ShapeDtyp...  19.6 us
    unnamed x1, local copies, waits for them, and re-layouts  1.77 us

profile of v5, /device:TPU:1, one launch (start us, length us, event | category | flops | bytes accessed | tf_op | source)
XLA Modules:
  0.0 21.4 jit_solution(3856808583707975222)
XLA Ops:
  0.0 19.6 %shard_map.46 = f32[3,128,256]{2,1,0:T(8,128)} custom-call(f32[512,128]{1,0:T(8,128)} %slab_hbm.1, f32[512,256]{1,0:T(8,128)} %orb_hbm.1, f32[3,2,64,64]{3,2,1,0:T(8,128)} %ops_hbm.1, f32[3,512]{1,0:T(4,128)} %wt_hbm.1), custom_call_target="tpu_custom_call" | custom-call | flops 402653184 | bytes 2097152 | tf_op jit(solution)/shard_map/pallas_call | solution.py:229
  19.6 1.8 %copy.6 = f32[3,128,256]{2,1,0:T(8,128)} copy(f32[3,128,256]{2,1,0:T(8,128)} %shard_map.46) | data formatting | bytes 786432
